TPU v7x, 512 devices: a whole 4x8x8 slice. The times are simulated.
512 devices in a mesh: rep: 16 (over y_hi, x, core), fsdp: 32 (over z, y_lo).
Axes of the slice: x: 4, y: 8 (y_hi: 2, y_lo: 4; y = y_hi * 4 + y_lo), z: 8, core: 2. Of those that a mesh axis runs over, the one named last changes fastest.
Arguments:
- grads: float32 [16, 256, 16384], P('rep', 'fsdp'), may hold values from -6 to 6
- master: float32 [256, 16384], P('fsdp'), may hold values from -6 to 6
- moment_one: float32 [256, 16384], P('fsdp'), may hold values from -2 to 2
- moment_two: float32 [256, 16384], P('fsdp'), may hold values from 0.05 to 2
Outputs:
- new_master: float32 [256, 16384], P('fsdp')
- new_one: float32 [256, 16384], P('fsdp')
- new_two: float32 [256, 16384], P('fsdp')
- rollout: bfloat16 [256, 16384], P(None, 'fsdp')
All inputs are finite; a program needn't handle non-finite values.
Results may differ from a plain program's by a relative error of at most 0.0025.
Values may be sent and summed in bfloat16 or wider, within the bound.
No kernel may reach another device: no remote copies, remote signals or barrier semaphores. Data moves between devices by JAX's collectives and lax.ppermute only.
A program may use at most 64 MiB of HBM per device.

v0:
```python
import jax
import jax.numpy as jnp
from jax import lax
from jax.sharding import PartitionSpec as P

STEP = 10


def adamw(mean_grad, master, moment_one, moment_two):
    new_one = 0.9 * moment_one + 0.1 * mean_grad
    new_two = 0.95 * moment_two + 0.05 * mean_grad * mean_grad
    corrected_one = new_one / (1.0 - 0.9**STEP)
    corrected_two = new_two / (1.0 - 0.95**STEP)
    new_master = master - 0.02 * (corrected_one / (jnp.sqrt(corrected_two) + 1e-08) + 0.1 * master)
    return (new_master, new_one, new_two)


def local(grads, master, moment_one, moment_two):
    row_count, full_width = master.shape
    fsdp_count = lax.axis_size("fsdp")
    rep_count = lax.axis_size("rep")
    piece_width = full_width // fsdp_count
    block_count = 1
    block_width = piece_width // block_count

    def columns(source):
        viewed = source.reshape(row_count, fsdp_count, piece_width)
        return viewed.reshape(row_count, fsdp_count * block_width)

    masters, firsts, seconds, rollouts = ([], [], [], [])
    grad_block = columns(grads[0])
    master_block = columns(master)
    first_block = columns(moment_one)
    second_block = columns(moment_two)
    mean_grad = lax.psum(grad_block.astype(jnp.bfloat16), "rep").astype(jnp.float32) / rep_count
    new_master, new_one, new_two = adamw(mean_grad, master_block, first_block, second_block)
    fresh = lax.all_to_all(
        new_master.astype(jnp.bfloat16), "fsdp", split_axis=1, concat_axis=0, tiled=True
    )
    masters.append(new_master.reshape(row_count, fsdp_count, block_width))
    firsts.append(new_one.reshape(row_count, fsdp_count, block_width))
    seconds.append(new_two.reshape(row_count, fsdp_count, block_width))
    rollouts.append(fresh)

    def assemble(pieces):
        return pieces[0].reshape(row_count, full_width)

    rollout = rollouts[0]
    return (assemble(masters), assemble(firsts), assemble(seconds), rollout)


def solution(mesh):
    placed = (P("rep", "fsdp", None), P("fsdp", None), P("fsdp", None), P("fsdp", None))
    return jax.shard_map(
        local,
        mesh=mesh,
        in_specs=placed,
        out_specs=(P("fsdp", None), P("fsdp", None), P("fsdp", None), P(None, "fsdp")),
        check_vma=False,
    )
```

profile of v0, /device:TPU:7, one launch (start us, length us, event | category | flops | bytes accessed | tf_op | source)
XLA Modules:
  0.0 229.1 jit_solution(11922680237035600617)
XLA Ops:
  7.2 0.0 copy-start.1
  7.2 0.0 copy-start
  7.2 0.0 all-reduce.2.cloned.1.call-start
  7.2 1.8 convert_bitcast_fusion
  9.1 0.0 all-reduce.2.cloned.1.call-update
  9.1 189.1 %all-reduce.2.cloned.1.call-done = bf16[8,16384]{1,0:T(8,128)(2,1)} async-done(((bf16[8,16384]{1,0:T(8,128)(2,1)}), bf16[8,16384]{1,0:T(8,128)(2,1)}) %all-reduce.2.cloned.1.call-update) | async-done | bytes 262160 | tf_op jit(solution)/shard_map/psum | solution.py:35
  198.2 0.0 copy-done.1
  198.2 0.0 copy-done
  198.2 2.5 %fusion.3 = (bf16[8,16384]{1,0:T(8,128)(2,1)S(1)}, f32[8,16384]{1,0:T(8,128)}, f32[8,16384]{1,0:T(8,128)}, f32[8,16384]{1,0:T(8,128)}) fusion(f32[8,16384]{1,0:T(8,128)S(1)} %copy-done, bf16[8,16384]{1,0:T(8,128)(2,1)} %all-reduce.2.cloned.1.call-done, f32[8,16384]{1,0:T(8,128)S(1)} %copy-done.1, f32[8,16384]{1,0:T(8,128)} %param.7), kind=kLoop, calls=%fused_computation.8 | loop fusion | flops 2359296 | bytes 3670016 | tf_op jit(solution)/shard_map/convert_element_type | solution.py:38
  200.8 20.8 %all_to_all.19 = bf16[8,32,512]{2,0,1:T(8,128)(2,1)S(1)} all-to-all(bf16[8,32,512]{2,0,1:T(8,128)(2,1)S(1)} %bitcast.6), channel_id=1, replica_groups=mesh['rep'=16,'fsdp'=32] {'fsdp'}, dimensions={1} | all-to-all | bytes 524288 | tf_op jit(solution)/shard_map/all_to_all | solution.py:37
  221.6 0.7 copy.10
Async XLA Ops:
  7.2 191.1 %copy-start.1 = (f32[8,16384]{1,0:T(8,128)S(1)}, f32[8,16384]{1,0:T(8,128)}, u32[]{:S(2)}) copy-start(f32[8,16384]{1,0:T(8,128)} %param.6) | copy-start | bytes 1572868
  7.2 191.0 %copy-start = (f32[8,16384]{1,0:T(8,128)S(1)}, f32[8,16384]{1,0:T(8,128)}, u32[]{:S(2)}) copy-start(f32[8,16384]{1,0:T(8,128)} %param.5) | copy-start | bytes 1572868
  7.2 191.0 %all-reduce.2.cloned.1.call-start = ((), (), s32[]{:S(2)}) async-start(), calls=%async_computation.1 | async-start | bytes 524288 | tf_op jit(solution)/shard_map/psum | solution.py:35
Sparse Core Ops, SparseCore 0:
  11.5 186.6 all-reduce.1
where the time goes:
time: 229 us
  waiting for transfers between devices  189 us (83%)
  blocking collectives  20.8 us (9%)
  between operations  14 us (6%)
  other arithmetic  4.38 us (2%)
    psum x1, waiting for transfers between devices, local(): lax.psum(grad_block.astype(jnp.bfloat16), 'rep').astype(jnp.float32)  189 us
    all_to_all x1, blocking collectives, local(): lax.all_to_all(new_master.astype(jnp.bfloat16), 'fsdp', split_axis=1, con...  20.8 us
  transfers between devices with their start and end apart: 1, of which 1 were waited for; matrix products, arithmetic and copies ran while one was open for 0% of the time, Pallas kernels for 0%

commit v1 on v0

--- a/solution.py
+++ b/solution.py
@@ -32,7 +32,12 @@
     master_block = columns(master)
     first_block = columns(moment_one)
     second_block = columns(moment_two)
-    mean_grad = lax.psum(grad_block.astype(jnp.bfloat16), "rep").astype(jnp.float32) / rep_count
+    mean_grad = (
+        lax.all_gather(grad_block.astype(jnp.bfloat16), axis_name="rep")
+        .sum(axis=0)
+        .astype(jnp.float32)
+        / rep_count
+    )
     new_master, new_one, new_two = adamw(mean_grad, master_block, first_block, second_block)
     fresh = lax.all_to_all(
         new_master.astype(jnp.bfloat16), "fsdp", split_axis=1, concat_axis=0, tiled=True

time: 229 us -> 132 us (0.58)
  waiting for transfers between devices: 189 us -> 90 us
    psum x1 -> x0, waiting for transfers between devices: 189 us -> none  [local(): lax.psum(grad_block.astype(jnp.bfloat16), 'rep').astype(jnp.float32)]
    all_gather x0 -> x1, waiting for transfers between devices: none -> 90 us  [local(): lax.all_gather(grad_block.astype(jnp.bfloat16), axis_name='rep').sum(axis=0)]
    reduce_sum x0 -> x1, other arithmetic: none -> 2.86 us  [local(): mean_grad = lax.all_gather(grad_block.astype(jnp.bfloat16), axis_name='re...]
where the time goes in v1:
time: 132 us; the launch traced here: 130 us
  waiting for transfers between devices  90 us (68%)
  blocking collectives  19 us (14%)
  between operations  14.1 us (11%)
  other arithmetic  6.14 us (5%)
    all_gather x1, waiting for transfers between devices, local(): lax.all_gather(grad_block.astype(jnp.bfloat16), axis_name='rep').sum(axis=0)  90 us
    all_to_all x1, blocking collectives, local(): lax.all_to_all(new_master.astype(jnp.bfloat16), 'fsdp', split_axis=1, con...  19 us
    reduce_sum x1, other arithmetic, local(): mean_grad = lax.all_gather(grad_block.astype(jnp.bfloat16), axis_name='re...  2.86 us
  transfers between devices with their start and end apart: 1, of which 1 were waited for; matrix products, arithmetic and copies ran while one was open for 0% of the time, Pallas kernels for 0%

profile of v1, /device:TPU:7, one launch (start us, length us, event | category | flops | bytes accessed | tf_op | source)
XLA Modules:
  0.0 130.1 jit_solution(13178251562014390095)
XLA Ops:
  7.2 0.0 copy-start.2
  7.2 0.0 copy-start.1
  7.2 0.0 copy-start
  7.2 0.0 all-gather.2.cloned.1.call-start
  7.2 1.9 %convert_element_type.12 = bf16[1,8,16384]{2,1,0:T(8,128)(2,1)} convert(f32[1,8,16384]{2,1,0:T(8,128)} %param.4) | non-fusion elementwise | flops 131072 | bytes 786432 | tf_op jit(solution)/shard_map/convert_element_type | solution.py:36
  9.1 0.0 all-gather.2.cloned.1.call-update
  9.1 90.0 %all-gather.2.cloned.1.call-done = bf16[16,8,16384]{2,1,0:T(8,128)(2,1)} async-done(((bf16[1,8,16384]{2,1,0:T(8,128)(2,1)}), bf16[16,8,16384]{2,1,0:T(8,128)(2,1)}) %all-gather.2.cloned.1.call-update) | async-done | bytes 4194320 | tf_op jit(solution)/shard_map/all_gather | solution.py:36
  99.2 2.9 %reduce_sum.12 = bf16[8,16384]{1,0:T(8,128)(2,1)S(1)} reduce(bf16[16,8,16384]{2,1,0:T(8,128)(2,1)} %all-gather.2.cloned.1.call-done, bf16[]{:T(256)} %constant.7.clone.1), dimensions={0}, to_apply=%region_0.0 | reduce | flops 1966080 | bytes 4456450 | tf_op jit(solution)/shard_map/reduce_sum | solution.py:37
  102.0 0.0 copy-done.2
  102.0 0.0 copy-done.1
  102.0 0.0 copy-done
  102.1 1.4 %fusion.3 = (bf16[8,16384]{1,0:T(8,128)(2,1)S(1)}, f32[8,16384]{1,0:T(8,128)}, f32[8,16384]{1,0:T(8,128)}, f32[8,16384]{1,0:T(8,128)}) fusion(f32[8,16384]{1,0:T(8,128)S(1)} %copy-done, bf16[8,16384]{1,0:T(8,128)(2,1)S(1)} %reduce_sum.12, f32[8,16384]{1,0:T(8,128)S(1)} %copy-done.1, f32[8,16384]{1,0:T(8,128)S(1)} %copy-done.2), kind=kLoop, calls=%fused_computation.7 | loop fusion | flops 2359296 | bytes 3670016 | tf_op jit(solution)/shard_map/convert_element_type | solution.py:43
  103.5 19.0 %all_to_all.19 = bf16[8,32,512]{2,0,1:T(8,128)(2,1)S(1)} all-to-all(bf16[8,32,512]{2,0,1:T(8,128)(2,1)S(1)} %bitcast.4), channel_id=1, replica_groups=mesh['rep'=16,'fsdp'=32] {'fsdp'}, dimensions={1} | all-to-all | bytes 524288 | tf_op jit(solution)/shard_map/all_to_all | solution.py:42
  122.5 0.7 copy.9
Async XLA Ops:
  7.2 94.9 %copy-start.2 = (f32[8,16384]{1,0:T(8,128)S(1)}, f32[8,16384]{1,0:T(8,128)}, u32[]{:S(2)}) copy-start(f32[8,16384]{1,0:T(8,128)} %param.7) | copy-start | bytes 1572868
  7.2 94.9 %copy-start.1 = (f32[8,16384]{1,0:T(8,128)S(1)}, f32[8,16384]{1,0:T(8,128)}, u32[]{:S(2)}) copy-start(f32[8,16384]{1,0:T(8,128)} %param.6) | copy-start | bytes 1572868
  7.2 94.9 %copy-start = (f32[8,16384]{1,0:T(8,128)S(1)}, f32[8,16384]{1,0:T(8,128)}, u32[]{:S(2)}) copy-start(f32[8,16384]{1,0:T(8,128)} %param.5) | copy-start | bytes 1572868
  7.2 92.0 %all-gather.2.cloned.1.call-start = ((), (), s32[]{:S(2)}) async-start(), calls=%async_computation.1 | async-start | bytes 4456448 | tf_op jit(solution)/shard_map/all_gather | solution.py:36
Sparse Core Ops, SparseCore 0:
  11.9 87.1 all-gather.1

commit v2 on v0

--- a/solution.py
+++ b/solution.py
@@ -1,9 +1,26 @@
+import functools
 import jax
 import jax.numpy as jnp
 from jax import lax
 from jax.sharding import PartitionSpec as P
 
 STEP = 10
+
+
+def connect_the_zones(x_part, array_axis, pos_dim):
+    value_now = jnp.concatenate(
+        lax.all_to_all(
+            jnp.stack(jnp.split(x_part, lax.axis_size("fsdp"), axis=array_axis)),
+            axis_name="fsdp",
+            concat_axis=0,
+            split_axis=0,
+        ),
+        axis=pos_dim,
+    )
+    return value_now
+
+
+load_forms = functools.partial(connect_the_zones, array_axis=1, pos_dim=0)
 
 
 def adamw(mean_grad, master, moment_one, moment_two):
@@ -34,9 +51,7 @@
     second_block = columns(moment_two)
     mean_grad = lax.psum(grad_block.astype(jnp.bfloat16), "rep").astype(jnp.float32) / rep_count
     new_master, new_one, new_two = adamw(mean_grad, master_block, first_block, second_block)
-    fresh = lax.all_to_all(
-        new_master.astype(jnp.bfloat16), "fsdp", split_axis=1, concat_axis=0, tiled=True
-    )
+    fresh = load_forms(new_master.astype(jnp.bfloat16))
     masters.append(new_master.reshape(row_count, fsdp_count, block_width))
     firsts.append(new_one.reshape(row_count, fsdp_count, block_width))
     seconds.append(new_two.reshape(row_count, fsdp_count, block_width))

time: 229 us -> 230 us (level)
  no operation moved by 1% of the time
where the time goes in v2:
time: 230 us; the launch traced here: 229 us
  waiting for transfers between devices  189 us (82%)
  blocking collectives  20.8 us (9%)
  between operations  14.3 us (6%)
  other arithmetic  4.38 us (2%)
    psum x1, waiting for transfers between devices, local(): lax.psum(grad_block.astype(jnp.bfloat16), 'rep').astype(jnp.float32)  189 us
    all_to_all x1, blocking collectives, connect_the_zones(): lax.all_to_all(jnp.stack(jnp.split(x_part, lax.axis_size('fsdp'), axis=ar...  20.8 us
  transfers between devices with their start and end apart: 1, of which 1 were waited for; matrix products, arithmetic and copies ran while one was open for 0% of the time, Pallas kernels for 0%

profile of v2, /device:TPU:7, one launch (start us, length us, event | category | flops | bytes accessed | tf_op | source)
XLA Modules:
  0.0 229.5 jit_solution(13532089674537964376)
XLA Ops:
  7.2 0.0 copy-start.1
  7.2 0.0 copy-start
  7.2 0.0 all-reduce.2.cloned.1.call-start
  7.2 1.8 convert_bitcast_fusion
  9.1 0.0 all-reduce.2.cloned.1.call-update
  9.1 189.1 %all-reduce.2.cloned.1.call-done = bf16[8,16384]{1,0:T(8,128)(2,1)} async-done(((bf16[8,16384]{1,0:T(8,128)(2,1)}), bf16[8,16384]{1,0:T(8,128)(2,1)}) %all-reduce.2.cloned.1.call-update) | async-done | bytes 262160 | tf_op jit(solution)/shard_map/psum | solution.py:52
  198.2 0.0 copy-done.1
  198.2 0.0 copy-done
  198.2 2.5 %fusion.3 = (bf16[8,16384]{1,0:T(8,128)(2,1)S(1)}, f32[8,16384]{1,0:T(8,128)}, f32[8,16384]{1,0:T(8,128)}, f32[8,16384]{1,0:T(8,128)}) fusion(f32[8,16384]{1,0:T(8,128)S(1)} %copy-done, bf16[8,16384]{1,0:T(8,128)(2,1)} %all-reduce.2.cloned.1.call-done, f32[8,16384]{1,0:T(8,128)S(1)} %copy-done.1, f32[8,16384]{1,0:T(8,128)} %param.7), kind=kLoop, calls=%fused_computation.72 | loop fusion | flops 2359296 | bytes 3670016 | tf_op jit(solution)/shard_map/convert_element_type | solution.py:54
  201.1 20.8 %all_to_all.5 = bf16[32,8,512]{2,1,0:T(8,128)(2,1)S(1)} all-to-all(bf16[32,8,512]{2,1,0:T(8,128)(2,1)S(1)} %constant_dynamic-update-slice_fusion), channel_id=1, replica_groups=mesh['rep'=16,'fsdp'=32] {'fsdp'}, dimensions={0} | all-to-all | bytes 524288 | tf_op jit(solution)/shard_map/all_to_all | solution.py:12
  221.9 0.7 copy.41
  (32 shorter events, 0.1 us)
Async XLA Ops:
  7.2 191.1 %copy-start.1 = (f32[8,16384]{1,0:T(8,128)S(1)}, f32[8,16384]{1,0:T(8,128)}, u32[]{:S(2)}) copy-start(f32[8,16384]{1,0:T(8,128)} %param.6) | copy-start | bytes 1572868
  7.2 191.0 %copy-start = (f32[8,16384]{1,0:T(8,128)S(1)}, f32[8,16384]{1,0:T(8,128)}, u32[]{:S(2)}) copy-start(f32[8,16384]{1,0:T(8,128)} %param.5) | copy-start | bytes 1572868
  7.2 191.0 %all-reduce.2.cloned.1.call-start = ((), (), s32[]{:S(2)}) async-start(), calls=%async_computation.1 | async-start | bytes 524288 | tf_op jit(solution)/shard_map/psum | solution.py:52
Sparse Core Ops, SparseCore 0:
  11.5 186.6 all-reduce.1
